TPU v7x, 32 devices: a whole 2x2x4 slice. The times are simulated.
32 devices in a mesh: grp: 4 (over y, core), row: 8 (over z, x).
Axes of the slice: x: 2, y: 2, z: 4, core: 2. Of those that a mesh axis runs over, the one named last changes fastest.
Arguments:
- features: bfloat16 [12288, 2048], P(('grp', 'row'))
- clip_starts: int32 [64], replicated, may hold values from 0 to 12286, as said below
- kernel_one: bfloat16 [576, 128], P('row', 'grp'), may hold values from -0.25 to 0.25
- kernel_two: bfloat16 [1152, 128], P('row', 'grp'), may hold values from -0.1875 to 0.1875
- gain_one: bfloat16 [128], P('grp'), may hold values from 0.099609375 to 1.8984375
- shift_one: bfloat16 [128], P('grp'), may hold values from -3 to 3
- gain_two: bfloat16 [128], P('grp'), may hold values from 0.099609375 to 1.8984375
- shift_two: bfloat16 [128], P('grp'), may hold values from -3 to 3
- cotangent: bfloat16 [6144, 2048], P(('grp', 'row'))
Outputs:
- block_out: bfloat16 [6144, 2048], P(('grp', 'row'))
- grad_features: float32 [12288, 2048], P(('grp', 'row'))
- grad_kernel_one: float32 [576, 128], P('row', 'grp')
- grad_kernel_two: float32 [1152, 128], P('row', 'grp')
- grad_gain_one: float32 [128], P('grp')
- grad_shift_one: float32 [128], P('grp')
- grad_gain_two: float32 [128], P('grp')
- grad_shift_two: float32 [128], P('grp')
Inputs may be any that keep to these rules, and one draw needn't show every extreme that they name: `clip_starts`: clip starts increase and are even; the first is 0 and the last is 12286; exactly two fall in each block of 384 frames, and no other lies on a block's first frame.
All inputs are finite; a program needn't handle non-finite values.
Results may differ from a plain program's by a relative error of at most 0.015.
Values may be sent and summed in bfloat16 or wider, within the bound.
No kernel may reach another device: no remote copies, remote signals or barrier semaphores. Data moves between devices by JAX's collectives and lax.ppermute only.
A program may use at most 192 MiB of HBM per device.

v0:
```python
import jax
import jax.numpy as jnp
from jax import lax
from jax.experimental import pallas as pl
from jax.experimental.pallas import tpu as pltpu
from jax.sharding import PartitionSpec as P

MEL = 32
C_IN = 64
C_MID = 128
EPS = 1e-05
AXES = ("grp", "row")
LANES = 128
TAIL = 16
WIDE = 4 * LANES
BOTH = 2 * C_MID
F32 = jnp.float32
BF16 = jnp.bfloat16
TILE = 16
SIDES = 4
MIB = 2**20

VMEM = pl.BlockSpec(memory_space=pltpu.VMEM)
ANY = pl.BlockSpec(memory_space=pl.ANY)
HBM = pl.BlockSpec(memory_space=pltpu.HBM)


def like(shape, dtype):
    return jax.ShapeDtypeStruct(shape, dtype)


def call(body, args, outs, scratch=(), limit=14, in_specs=None, out_specs=None, **more):
    return pl.pallas_call(
        body,
        in_specs=in_specs or [VMEM] * len(args),
        out_specs=out_specs or [VMEM] * len(outs),
        out_shape=outs,
        scratch_shapes=list(scratch),
        compiler_params=pltpu.CompilerParams(vmem_limit_bytes=limit * MIB),
        cost_estimate=pl.CostEstimate(flops=5 * 10**9, bytes_accessed=0, transcendentals=0),
        **more,
    )(*args)


def padded(size):
    return -(-size // LANES) * LANES


def packed_rows(share, wide):
    rest = wide - LANES
    if rest > 0 and share == 32 and 3 * (LANES - rest) >= rest:
        return share + 24
    return share * (padded(wide) // LANES)


def pack(block, rows):
    share, wide = block.shape
    if rows % share == 0:
        block = jnp.concatenate([block, jnp.zeros((share, padded(wide) - wide), F32)], axis=1)
        return jnp.concatenate(
            [block[:, at : at + LANES] for at in range(0, block.shape[1], LANES)], axis=0
        )
    rest = block[:, LANES:]
    room = 2 * LANES - wide
    tail = jnp.concatenate(
        [rest[24:32], jnp.zeros((8, 3 * room - rest.shape[1]), F32)], axis=1
    )
    tail = jnp.concatenate([tail[:, k * room : (k + 1) * room] for k in range(3)], axis=0)
    return jnp.concatenate([block[:, :LANES], jnp.concatenate([rest[0:24], tail], axis=1)], axis=0)


def unpack(block, share, wide):
    rows = block.shape[0]
    if rows % share == 0:
        parts = [block[at : at + share] for at in range(0, rows, share)]
        return jnp.concatenate(parts, axis=1)[:, 0:wide]
    width = wide - LANES
    second = block[share:]
    tail = jnp.concatenate([second[8 * k : 8 * k + 8, width:] for k in range(3)], axis=1)
    rest = jnp.concatenate([second[:, :width], tail[:, :width]], axis=0)
    return jnp.concatenate([block[0:share], rest], axis=1)


def partial_sum(values):
    return jnp.sum(values.reshape(-1, 8, values.shape[-1]), axis=0)


def fold(values):
    total = jnp.sum(values, axis=0, keepdims=True)
    return total[:, :C_MID] + total[:, C_MID:]


def spread(first, second, out):
    sums = jnp.concatenate([first, second], axis=0)
    out[...] = jnp.broadcast_to(sums[None], out.shape)


def twice(row):
    return jnp.concatenate([row, row], axis=1)


def tiles(rows):
    return range(0, rows, TILE)


def emit_taps(taps, masks, evens, odds, tile_of):
    rows = masks.shape[1]
    kept = taps.shape[0]
    for r in tiles(rows):
        even, odd = tile_of(r)
        evens[r : r + TILE] = even
        odds[8 + r : 8 + r + TILE] = odd
        if r == 0:
            evens[rows : rows + 1] = even[0:1]
        if r + TILE == rows:
            odds[7:8] = odd[TILE - 1 : TILE]
        if r < kept:
            taps[r : r + TILE, 128:256] = even.astype(BF16)
            taps[r : r + TILE, 256:384] = odd.astype(BF16)
    for r in tiles(kept):
        span = slice(r, r + TILE)
        before = odds[7 + r : 7 + r + TILE] * masks[0, span]
        after = evens[1 + r : 1 + r + TILE] * masks[1, span]
        taps[span, 0:128] = before.astype(BF16)
        taps[span, 384:512] = after.astype(BF16)


def halves_of(value):
    return value[:, :C_MID], value[:, C_MID:]


def add_sums(acc, first, second):
    acc[0] += first
    acc[1] += second


def side_scratch(rows):
    return [pltpu.VMEM((rows + 8, LANES), F32)] * (2 * SIDES)


def stats_of(out, mels, rows, half, acc):
    first = jnp.zeros((8, BOTH), F32)
    second = jnp.zeros((8, BOTH), F32)
    for k in range(mels):
        for r in range(0, half, 8):
            value = out[k * rows + r : k * rows + r + 8]
            first += value
            second += value * value
    add_sums(acc, first, second)


def normed_sum(with_half_lifted, plain, gain, shift):
    return (2.0 * with_half_lifted - shift * plain) / gain


def stat_sums(stats):
    return jnp.sum(stats[...], axis=0)


def norm_terms(sums, count):
    mean = sums[0:1] / count
    rstd = lax.rsqrt(sums[1:2] / count - mean * mean + EPS)
    return mean, rstd


def dot_rows(first, second):
    return lax.dot_general(
        first, second, (((0,), (0,)), ((), ())), preferred_element_type=F32
    )


def ring_slot(ring, m):
    return ring[m % (len(ring) - 1)] if 0 <= m < MEL else ring[-1]


def stack(ring, mels, rows, lanes=slice(None)):
    return jnp.concatenate([ring_slot(ring, m)[0:rows, lanes] for m in mels], axis=0)


def ring_scratch(slots, rows):
    return [pltpu.VMEM((rows, WIDE), BF16)] * slots


def clear_ends(taps):
    blank = jnp.zeros(taps.shape[1:], BF16)
    taps[0] = blank
    taps[taps.shape[0] - 1] = blank


def setup_body(k1, k2, ga, sa, gb, sb, x_head, x_tail, c_head, c_tail, w_out, up, down):
    share = k1.shape[0]
    copies = w_out.shape[0]
    first = lax.broadcasted_iota(jnp.int32, (share, share), 0)
    second = lax.broadcasted_iota(jnp.int32, (share, share), 1)
    columns = [k1[...].astype(F32), k2[...].astype(F32)]
    for vector in (ga, sa, gb, sb):
        wide = jnp.broadcast_to(vector[...].astype(F32), (share, share))
        columns.append(jnp.sum(jnp.where(first == second, wide, 0.0), axis=1, keepdims=True))
    chunk = pack(jnp.concatenate(columns, axis=1), w_out.shape[1]).astype(BF16)
    for i in range(copies):
        w_out[i] = chunk
    row = lax.broadcasted_iota(jnp.int32, (8, x_head.shape[1]), 0)
    xt = x_tail[...].astype(F32)
    ct = c_tail[...].astype(F32)
    up[...] = jnp.where(
        row < 4, pltpu.roll(xt[8:16], 4, 0), jnp.where(row == 4, ct[15:16], 0.0)
    ).astype(BF16)
    xh = x_head[...].astype(F32)
    ch = c_head[...].astype(F32)
    down[...] = jnp.where(row < 4, xh[0:8], jnp.where(row == 4, ch[0:1], 0.0)).astype(BF16)


def setup(k1t, k2t, vectors, features, cotangent, copies):
    frames, wide = features.shape
    halves = cotangent.shape[0]
    share = k1t.shape[0]
    w = (copies, packed_rows(share, k1t.shape[1] + k2t.shape[1] + 4), LANES)
    whole = lambda shape: pl.BlockSpec(shape, lambda i: (0,) * len(shape))
    outs = [like(w, BF16), like((8, wide), BF16), like((8, wide), BF16)]
    return call(
        setup_body,
        (k1t, k2t, *vectors, features, features, cotangent, cotangent),
        outs,
        limit=56,
        in_specs=[
            whole(k1t.shape),
            whole(k2t.shape),
            *[whole((1, share))] * 4,
            pl.BlockSpec((16, wide), lambda i: (0, 0)),
            pl.BlockSpec((16, wide), lambda i: (frames // 16 - 1, 0)),
            pl.BlockSpec((16, wide), lambda i: (0, 0)),
            pl.BlockSpec((16, wide), lambda i: (halves // 16 - 1, 0)),
        ],
        out_specs=[whole(o.shape) for o in outs],
        grid=(1,),
    )


def emit_masks(copies, clips, masks):
    rows = masks.shape[1]
    half = rows - TAIL
    frames = 2 * half
    start = lax.axis_index(AXES) * frames
    place = lax.broadcasted_iota(jnp.int32, (rows, clips.shape[1]), 0)
    pair = jnp.where(place >= half + TAIL // 2, place - rows, place)
    frame = start + 2 * pair
    starts = jnp.broadcast_to(clips[...], (rows, clips.shape[1]))
    for slot, shift in ((0, 0), (1, 2)):
        hit = (frame + shift == starts) | (frame + shift >= frames * copies)
        begins = jnp.max(jnp.where(hit, 1.0, 0.0), axis=1, keepdims=True)
        masks[slot] = jnp.broadcast_to(1.0 - begins, (rows, LANES))


def split_bins(parts):
    low = lax.broadcasted_iota(jnp.int32, parts[0].shape, 1) < C_IN
    first, second = [], []
    for here, there in (parts[0:2], parts[2:4]):
        first.append(jnp.where(low, here, pltpu.roll(there, C_IN, 1)))
        second.append(jnp.where(low, pltpu.roll(here, C_IN, 1), there))
    return jnp.concatenate(first + second, axis=1)


def near_bins(taps, pairs, rows):
    left, mid, right = [
        jnp.concatenate([taps[1 + j + k, 0:rows] for j in pairs], axis=0) for k in (-1, 0, 1)
    ]
    first = jnp.concatenate([left[:, BOTH:], mid], axis=1)
    second = jnp.concatenate([mid, right[:, :BOTH]], axis=1)
    return jnp.concatenate([first, second], axis=0)


def taps_one_emitter(x, up, down, masks, taps, frames):
    rows = masks.shape[1]
    half = rows - TAIL
    clear_ends(taps)
    row = lax.broadcasted_iota(jnp.int32, (8, LANES), 0)
    lead = 24
    own = 2 * half
    for held in frames:
        held[0:16] = jnp.zeros((16, LANES), F32)
        held[lead + own + 8 : lead + own + 24] = jnp.zeros((16, LANES), F32)

    def pair(j):
        held = frames[j % len(frames)]
        lanes = slice(j * LANES, (j + 1) * LANES)
        u = up[:, lanes].astype(F32)
        d = down[:, lanes].astype(F32)
        held[lead - 8 : lead] = jnp.where(row >= 4, pltpu.roll(u, 4, 0), 0.0)
        held[lead + own : lead + own + 8] = jnp.where(row < 4, d, 0.0)
        for r in tiles(own):
            held[lead + r : lead + r + TILE] = x[r : r + TILE, lanes].astype(F32)

        def pick(first, count, shift):
            return held[pl.ds(lead + 2 * first + shift, count, stride=2), :]

        for r in tiles(rows):
            parts = []
            for shift in (-1, 0, 1, 2):
                if r < half:
                    parts.append(pick(r, TILE, shift))
                else:
                    parts.append(
                        jnp.concatenate([pick(half, 8, shift), pick(-8, 8, shift)], axis=0)
                    )
            span = slice(r, r + TILE)
            parts[0] = parts[0] * masks[0, span]
            parts[3] = parts[3] * masks[1, span]
            taps[1 + j, span, :] = split_bins(parts).astype(BF16)

    return pair


def conv_one_body(row_count, features, up, down, clips_in, wg,
                  pre, stats, taps, masks, k1_out, k2_out, vec_out, weight_two,
                  kf, weight, acc, x, clips, sems, clip_sem, *frames):
    clip_copy = pltpu.make_async_copy(clips_in, clips, clip_sem)
    clip_copy.start()
    wide = x.shape[1] // sems.shape[0]
    fetch = []
    for k in range(sems.shape[0]):
        lanes = pl.ds(k * wide, wide)
        fetch.append(pltpu.make_async_copy(features.at[:, lanes], x.at[:, lanes], sems.at[k]))
        fetch[k].start()
    clip_copy.wait()
    emit_masks(wg.shape[0], clips, masks)
    emit_pair = taps_one_emitter(x, up, down, masks, taps, frames)
    rows = taps.shape[1]
    half = rows - TAIL
    pairs = 2
    rows_one = 9 * C_IN // row_count
    rows_two = 9 * C_MID // row_count
    grps = wg.shape[0] // row_count
    share = C_MID // grps
    for r in range(row_count):
        shard = [
            unpack(wg[g * row_count + r].astype(F32), share, rows_one + rows_two + 4)
            for g in range(grps)
        ]
        shard = jnp.concatenate(shard, axis=0).T
        kf[rows_one * r : rows_one * (r + 1)] = shard[0:rows_one]
        at = 9 * C_IN + rows_two * r
        kf[at : at + rows_two] = shard[rows_one : rows_one + rows_two]
        if r == 0:
            vec_out[...] = shard[rows_one + rows_two : rows_one + rows_two + 4]
    k1_out[...] = kf[0 : 9 * C_IN].astype(BF16)
    k2_out[...] = kf[9 * C_IN :].astype(BF16)
    weight[...] = jnp.zeros(weight.shape, BF16)
    for d in range(3):
        for q in range(4):
            for p in range(2):
                t = q - p
                if 0 <= t < 3:
                    at = d * BOTH + q * C_IN
                    start = (3 * t + d) * C_IN
                    weight[at : at + C_IN, p * 128 : p * 128 + 128] = k1_out[start : start + C_IN]
    acc[...] = jnp.zeros(acc.shape, F32)

    def convolve(c):
        here = range(c * pairs, (c + 1) * pairs)
        out = jnp.dot(near_bins(taps, here, rows), weight[...], preferred_element_type=F32)
        for parity in range(2):
            for q in range(pairs):
                at = (parity * pairs + q) * rows
                pre[2 * (c * pairs + q) + parity] = out[at : at + rows]
        stats_of(out, 2 * pairs, rows, half, acc)

    total = MEL // 2
    for j in range(total):
        if j % (total // len(fetch)) == 0:
            fetch[j // (total // len(fetch))].wait()
        emit_pair(j)
        if j >= pairs and j % pairs == 0:
            convolve(j // pairs - 1)
        if j == 4:
            place_two(k2_out, weight_two)
    convolve(total // pairs - 1)
    spread(fold(acc[0]), fold(acc[1]), stats)


def conv_one(features, up, down, clips, wg, row_count):
    rows = features.shape[0] // 2 + TAIL
    copies = wg.shape[0]
    return call(
        lambda *refs: conv_one_body(row_count, *refs),
        (features, up, down, clips, wg),
        [
            like((MEL, rows, BOTH), F32),
            like((copies, 2, C_MID), F32),
            like((MEL // 2 + 2, rows, WIDE), BF16),
            like((2, rows, LANES), F32),
            like((9 * C_IN, C_MID), BF16),
            like((9 * C_MID, C_MID), BF16),
            like((4, C_MID), F32),
            like((3 * WIDE, BOTH), BF16),
        ],
        [
            pltpu.VMEM((9 * (C_IN + C_MID), C_MID), F32),
            pltpu.VMEM((3 * BOTH, BOTH), BF16),
            pltpu.VMEM((2, 8, BOTH), F32),
            pltpu.VMEM(features.shape, BF16),
            pltpu.VMEM(clips.shape, jnp.int32),
            pltpu.SemaphoreType.DMA((4,)),
            pltpu.SemaphoreType.DMA,
            *[pltpu.VMEM((features.shape[0] + 48, LANES), F32)] * 4,
        ],
        in_specs=[HBM, VMEM, VMEM, HBM, VMEM],
    )


def place_two(k2, weight):
    weight[...] = jnp.zeros(weight.shape, BF16)
    for d in range(3):
        for q in range(4):
            for p in range(2):
                t = q - p
                if 0 <= t < 3:
                    at = d * WIDE + q * 128
                    start = (3 * t + d) * C_MID
                    weight[at : at + 128, p * 128 : p * 128 + 128] = k2[start : start + C_MID]


def place_two_back(k2, weight):
    weight[...] = jnp.zeros(weight.shape, BF16)
    for t in range(3):
        for d in range(3):
            start = (3 * t + d) * C_MID
            turned = (0.5 * k2[start : start + C_MID].astype(F32).T).astype(BF16)
            for p in range(2):
                at = (2 - d) * WIDE + (2 - t + p) * 128
                weight[at : at + 128, p * 128 : p * 128 + 128] = turned


def place_one_back(k1, weight):
    weight[...] = jnp.zeros(weight.shape, BF16)
    for t in range(3):
        for d in range(3):
            start = (3 * t + d) * C_IN
            turned = k1[start : start + C_IN].astype(F32).T.astype(BF16)
            for mo in (1, 2):
                for p in range(2):
                    at = (mo - d + 1) * WIDE + (2 - t + p) * 128
                    to = p * 128 + (mo - 1) * 64
                    weight[at : at + 128, to : to + 64] = turned


def conv_two_body(count, pre_one, stats_one, vec, masks, k2, weight,
                  pre, stats, taps, sums_out, weight_back, acc, *sides):
    rows = masks.shape[1]
    half = rows - TAIL
    mels = 2
    sums = stat_sums(stats_one)
    sums_out[...] = sums
    mean, rstd = norm_terms(sums, count)
    scale = 0.5 * vec[0:1] * rstd
    shift = twice(0.5 * vec[1:2] - mean * scale)
    scale = twice(scale)
    clear_ends(taps)
    acc[...] = jnp.zeros(acc.shape, F32)

    def activate(m):
        def tile(r):
            h = pre_one[m, r : r + TILE] * scale + shift
            return halves_of(h + h * jnp.tanh(h))

        emit_taps(taps.at[1 + m], masks, sides[m % SIDES], sides[SIDES + m % SIDES], tile)

    def convolve(c):
        lhs = [taps[c * mels + d : (c + 1) * mels + d].reshape(mels * rows, WIDE) for d in range(3)]
        out = jnp.dot(jnp.concatenate(lhs, axis=1), weight[...], preferred_element_type=F32)
        pre[c * mels : (c + 1) * mels] = out.reshape(mels, rows, BOTH)
        stats_of(out, mels, rows, half, acc)

    for m in range(MEL):
        activate(m)
        if m >= mels and m % mels == 0:
            convolve(m // mels - 1)
        if m == 8:
            place_two_back(k2, weight_back)
    convolve(MEL // mels - 1)
    spread(fold(acc[0]), fold(acc[1]), stats)


def conv_two(pre_one, stats_one, vec, masks, k2, weight, count):
    copies = stats_one.shape[0]
    rows = masks.shape[1]
    return call(
        lambda *refs: conv_two_body(count, *refs),
        (pre_one, stats_one, vec, masks, k2, weight),
        [
            like((MEL, rows, BOTH), F32),
            like((copies, 2, C_MID), F32),
            like((MEL + 2, rows, WIDE), BF16),
            like((2, C_MID), F32),
            like((3 * WIDE, BOTH), BF16),
        ],
        [pltpu.VMEM((2, 8, BOTH), F32), *side_scratch(rows)],
    )


def norm_two_body(count, pre, stats_two, vec, cot, up, down, pooled, lift, back_stats, sums_out, acc):
    half = cot.shape[0]
    sums = stat_sums(stats_two)
    sums_out[...] = sums
    mean, rstd = norm_terms(sums, count)
    scale = 0.5 * vec[2:3] * rstd
    shift = 0.5 * vec[3:4] - mean * scale
    acc[...] = jnp.zeros(acc.shape, F32)
    row = lax.broadcasted_iota(jnp.int32, (TAIL, LANES), 0)

    factor = 0.125 * vec[2:3] * rstd

    def pair(j):
        lanes = pl.ds(pl.multiple_of(j * LANES, LANES), LANES)
        u = up[:, lanes].astype(F32)
        d = down[:, lanes].astype(F32)
        first = jnp.zeros((8, LANES), F32)
        second = jnp.zeros((8, LANES), F32)
        for r in tiles(half + TAIL):
            span = slice(r, r + TILE)
            if r < half:
                grad = cot[span, lanes].astype(F32) * factor
            else:
                grad = jnp.where(row == 0, d[4:5], jnp.where(row == TAIL - 1, u[4:5], 0.0)) * factor
            total = jnp.zeros((TILE, LANES), F32)
            for m in (2 * j, 2 * j + 1):
                for p in range(2):
                    side = slice(p * C_MID, (p + 1) * C_MID)
                    value = pre[m, span, side]
                    h = value * scale + shift
                    th = jnp.tanh(h)
                    one = 1.0 + th
                    silu = h * one
                    gl = grad * (one + (silu - silu * th))
                    lift[m, span, side] = gl
                    if r < half:
                        total += silu
                        first += partial_sum(gl)
                        second += partial_sum(gl * h)
            if r < half:
                pooled[span, lanes] = (total * 0.25).astype(BF16)
        add_sums(acc, first, second)

    def four_pairs(i, carry):
        for k in range(4):
            pair(4 * i + k)
        return carry

    lax.fori_loop(0, MEL // 8, four_pairs, 0)
    first, second = [jnp.sum(acc[k], axis=0, keepdims=True) for k in range(2)]
    scaled = vec[2:3] * rstd
    first = first / scaled
    spread(first, normed_sum(second / scaled, first, vec[2:3], vec[3:4]), back_stats)


def norm_two(pre, stats_two, vec, cot, up, down, count):
    copies = stats_two.shape[0]
    half, wide = cot.shape
    return call(
        lambda *refs: norm_two_body(count, *refs),
        (pre, stats_two, vec, cot, up, down),
        [
            like((half, wide), BF16),
            like((MEL, half + TAIL, BOTH), F32),
            like((copies, 2, C_MID), F32),
            like((2, C_MID), F32),
        ],
        [pltpu.VMEM((2, 8, LANES), F32)],
    )


def grad_terms(sums, back, gain, count):
    mean, rstd = norm_terms(sums, count)
    a = gain * rstd
    b = -a * rstd * (back[1:2] / count)
    c = -a * (back[0:1] / count) - b * mean
    return twice(a), twice(b), twice(c)


def back_two_body(count, lift, pre_two, sums_two, back_stats, vec, masks, weight, pre_one, sums_one,
                  taps_a, lift_one, two, back_out, sums_out, acc, acc_two, turned, *buffers):
    sides, taps = buffers[: 2 * SIDES], buffers[2 * SIDES :]
    rows = masks.shape[1]
    half = rows - TAIL
    mels = 1
    wide_mels = 4
    back = stat_sums(back_stats)
    sums_out[...] = back
    _, b, c = grad_terms(sums_two[...], back, vec[2:3], count)
    mean, rstd = norm_terms(sums_one[...], count)
    scale = 0.5 * vec[0:1] * rstd
    shift = twice(0.5 * vec[1:2] - mean * scale)
    scale = twice(scale)
    taps[-1][...] = jnp.zeros(taps[-1].shape, BF16)
    acc[...] = jnp.zeros(acc.shape, F32)

    def lower(m):
        def tile(r):
            span = slice(r, r + TILE)
            return halves_of(lift[m, span] + (pre_two[m, span] * b + c))

        emit_taps(ring_slot(taps, m), masks, sides[m % SIDES], sides[SIDES + m % SIDES], tile)

    def convolve(k):
        lhs = [ring_slot(taps, k + d - 1)[...] for d in range(3)]
        out = jnp.dot(jnp.concatenate(lhs, axis=1), weight[...], preferred_element_type=F32)
        first = jnp.zeros((8, BOTH), F32)
        second = jnp.zeros((8, BOTH), F32)
        for i in range(mels):
            m = k * mels + i
            for r in range(0, rows, 8):
                span = slice(r, r + 8)
                h = pre_one[m, span] * scale + shift
                th = jnp.tanh(h)
                one = 1.0 + th
                silu = h * one
                gl = out[i * rows + r : i * rows + r + 8] * (one + (silu - silu * th))
                lift_one[m, span] = gl
                if r < half:
                    first += gl
                    second += gl * h
        add_sums(acc, first, second)

    def correlate(k):
        here = range(k * wide_mels, (k + 1) * wide_mels)
        turned[...] = stack(taps, here, half, slice(128, 384)).T
        for d in range(3):
            first = here[0] + d
            near = taps_a[first : first + wide_mels, 0:half].reshape(wide_mels * half, WIDE)
            total = jnp.dot(turned[...], near, preferred_element_type=F32)
            lanes = slice(d * WIDE, (d + 1) * WIDE)
            if k == 0:
                acc_two[:, lanes] = total
            else:
                acc_two[:, lanes] += total

    for k in range(MEL // mels + 1):
        for m in range(k * mels, (k + 1) * mels):
            if m < MEL:
                lower(m)
        if k > 0:
            convolve(k - 1)
            if k * mels % wide_mels == 0:
                correlate(k * mels // wide_mels - 1)
    plain = fold(acc[0])
    spread(plain, normed_sum(fold(acc[1]), plain, vec[0:1], vec[1:2]), back_out)
    for t in range(3):
        for d in range(3):
            at = d * WIDE + t * 128
            to = (3 * t + d) * 128
            two[:, to : to + 128] = (
                acc_two[0:C_MID, at : at + 128] + acc_two[C_MID:BOTH, at + 128 : at + 256]
            )


def back_two(lift, pre_two, sums_two, back_stats, vec, masks, weight, pre_one, sums_one, taps_a, count):
    copies = back_stats.shape[0]
    rows = masks.shape[1]
    return call(
        lambda *refs: back_two_body(count, *refs),
        (lift, pre_two, sums_two, back_stats, vec, masks, weight, pre_one, sums_one, taps_a),
        [
            like((MEL, rows, BOTH), F32),
            like((C_MID, 9 * C_MID), F32),
            like((copies, 2, C_MID), F32),
            like((2, C_MID), F32),
        ],
        [
            pltpu.VMEM((2, 8, BOTH), F32),
            pltpu.VMEM((BOTH, 3 * WIDE), F32),
            pltpu.VMEM((BOTH, 4 * (rows - TAIL)), BF16),
            *side_scratch(rows),
            *ring_scratch(17, rows),
        ],

        input_output_aliases={0: 0},
    )


def scatter_blocks(out, parts, row_count):
    copies = out.shape[0]
    grps = copies // row_count
    share = C_MID // grps
    turned = [part.T for part in parts]
    sizes = [part.shape[1] // row_count for part in parts]
    for r in range(row_count):
        rows = [t[n * r : n * (r + 1)] for t, n in zip(turned, sizes)]
        back = jnp.concatenate(rows, axis=0).T
        for g in range(grps):
            block = back[share * g : share * (g + 1)]
            out[g * row_count + r] = pack(block, out.shape[1]).astype(BF16)


def kernel_one_step(taps_x, grads, acc, k, pairs):
    half = grads.shape[1] - TAIL
    here = range(k * pairs, (k + 1) * pairs)
    mels = [2 * j + parity for parity in range(2) for j in here]
    chosen = jnp.concatenate([grads[m, 0:half] for m in mels], axis=0)
    total = dot_rows(chosen, near_bins(taps_x, here, half))
    if k == 0:
        acc[...] = total
    else:
        acc[...] += total


def kernel_one_sums(acc):
    pieces = []
    for t in range(3):
        for d in range(3):
            total = jnp.zeros((C_MID, C_IN), F32)
            for p in range(2):
                at = d * BOTH + (t + p) * C_IN
                total += acc[p * C_MID : (p + 1) * C_MID, at : at + C_IN]
            pieces.append(total)
    return jnp.concatenate(pieces, axis=1)


STORED = 640


def grads_body(count, row_count, lift, pre_one, sums_one, back_stats, vec, masks, taps_x, two,
               stored, blocks, sums_out, acc_one, grads, low_masks, sems):
    back = stat_sums(back_stats)
    sums_out[...] = back
    a, b, c = grad_terms(sums_one[...], back, vec[0:1], count)
    rows = masks.shape[1]
    for slot in range(2):
        low_masks[:, slot * LANES : (slot + 1) * LANES] = masks[slot].astype(BF16)
    copies = [pltpu.make_async_copy(low_masks, stored.at[MEL], sems.at[sems.shape[0] - 1])]
    copies[0].start()

    def lower(m):
        for r in tiles(rows):
            span = slice(r, r + TILE)
            grads[m, span] = (lift[m, span] * a + (pre_one[m, span] * b + c)).astype(BF16)

    pairs = 2
    mels = 2 * pairs
    steps = MEL // mels
    for k in range(steps + 1):
        if k < steps:
            for m in range(mels * k, mels * (k + 1)):
                lower(m)
            here = pl.ds(mels * k, mels)
            copies.append(pltpu.make_async_copy(grads.at[here], stored.at[here], sems.at[k]))
            copies[-1].start()
        if k > 0:
            kernel_one_step(taps_x, grads, acc_one, k - 1, pairs)
    scatter_blocks(blocks, [kernel_one_sums(acc_one), two[...]], row_count)
    for copy in copies:
        copy.wait()


def kernel_grads(lift, pre_one, sums_one, back_stats, vec, masks, taps_x, two, row_count, count):
    copies = back_stats.shape[0]
    rows = masks.shape[1]
    share = C_MID * row_count // copies
    block_rows = packed_rows(share, 9 * (C_IN + C_MID) // row_count)
    return call(
        lambda *refs: grads_body(count, row_count, *refs),
        (lift, pre_one, sums_one, back_stats, vec, masks, taps_x, two),
        [
            like((STORED, rows, BOTH), BF16),
            like((copies, block_rows, LANES), BF16),
            like((2, C_MID), F32),
        ],
        [
            pltpu.VMEM((BOTH, 3 * BOTH), F32),
            pltpu.VMEM((MEL, rows, BOTH), BF16),
            pltpu.VMEM((rows, BOTH), BF16),
            pltpu.SemaphoreType.DMA((9,)),
        ],
        out_specs=[HBM, VMEM, VMEM],
    )


def features_body(stored, k1, out, grads, low_masks, masks, weight, woven, sems, out_sems, *buffers):
    sides, taps = buffers[: 2 * SIDES], buffers[2 * SIDES :]
    pairs = 4
    rows = grads.shape[1]
    half = rows - TAIL
    groups = sems.shape[0] - 1
    group = MEL // groups
    mask_copy = pltpu.make_async_copy(stored.at[MEL], low_masks, sems.at[groups])
    mask_copy.start()
    fetch = []
    for k in range(groups):
        here = pl.ds(k * group, group)
        fetch.append(pltpu.make_async_copy(stored.at[here], grads.at[here], sems.at[k]))
        fetch[k].start()
    taps[-1][...] = jnp.zeros(taps[-1].shape, BF16)
    place_one_back(k1, weight)
    mask_copy.wait()
    for slot in range(2):
        masks[slot] = low_masks[:, slot * LANES : (slot + 1) * LANES].astype(F32)

    def emit(m):
        def tile(r):
            return halves_of(grads[m, r : r + TILE].astype(F32))

        emit_taps(ring_slot(taps, m), masks, sides[m % SIDES], sides[SIDES + m % SIDES], tile)

    copies = []
    slots = woven.shape[0]

    def convolve(k):
        near = [
            stack(taps, [2 * (k * pairs + q) + i - 1 for q in range(pairs)], half) for i in range(4)
        ]
        part = jnp.dot(jnp.concatenate(near, axis=1), weight[...], preferred_element_type=F32)
        for q in range(pairs):
            j = k * pairs + q
            b = j % slots
            here = slice(q * half, (q + 1) * half)
            if j >= slots:
                copies[j - slots].wait()
            woven[b, pl.ds(0, half, stride=2), :] = part[here, 0:128]
            woven[b, pl.ds(1, half, stride=2), :] = part[here, 128:256]
            copy = pltpu.make_async_copy(
                woven.at[b], out.at[:, pl.ds(j * LANES, LANES)], out_sems.at[b]
            )
            copy.start()
            copies.append(copy)

    for m in range(MEL):
        if m % group == 0:
            fetch[m // group].wait()
        emit(m)
        if m > 0 and m % (2 * pairs) == 0:
            convolve(m // (2 * pairs) - 1)
    convolve(MEL // (2 * pairs) - 1)
    for copy in copies[-slots:]:
        copy.wait()


def features_grad(stored, k1):
    rows = stored.shape[1]
    half = rows - TAIL
    return call(
        features_body,
        (stored, k1),
        [like((2 * half, MEL * C_IN), F32)],
        [
            pltpu.VMEM((MEL, rows, BOTH), BF16),
            pltpu.VMEM((rows, BOTH), BF16),
            pltpu.VMEM((2, rows, LANES), F32),
            pltpu.VMEM((4 * WIDE, BOTH), BF16),
            pltpu.VMEM((8, 2 * half, LANES), F32),
            pltpu.SemaphoreType.DMA((9,)),
            pltpu.SemaphoreType.DMA((8,)),
            *side_scratch(rows),
            *ring_scratch(27, half),
        ],
        limit=24,
        in_specs=[HBM, VMEM],
        out_specs=[ANY],
    )[0]


def finish_body(got, back_one_sums, back_two_sums, own_one, own_two, ga, sa, gb, sb):
    size = own_one.shape[1]
    share = own_one.shape[0]
    total = jnp.sum(got[...].astype(F32), axis=0)
    total = unpack(total, share, size + own_two.shape[1])
    own_one[...] = total[:, 0:size]
    own_two[...] = total[:, size:]
    lane = lax.broadcasted_iota(jnp.int32, (share, C_MID), 1)
    row = lax.broadcasted_iota(jnp.int32, (share, C_MID), 0)
    chosen = lane == lax.axis_index("grp") * share + row
    first = lax.broadcasted_iota(jnp.int32, (share, share), 0)
    second = lax.broadcasted_iota(jnp.int32, (share, share), 1)
    for out, sums, k in (
        (ga, back_one_sums, 1), (sa, back_one_sums, 0), (gb, back_two_sums, 1), (sb, back_two_sums, 0)
    ):
        wide = jnp.broadcast_to(sums[k : k + 1], (share, C_MID))
        column = jnp.sum(jnp.where(chosen, wide, 0.0), axis=1, keepdims=True)
        wide = jnp.broadcast_to(column, (share, share))
        out[...] = jnp.sum(jnp.where(first == second, wide, 0.0), axis=0, keepdims=True)


def finish(got, back_one_sums, back_two_sums, share, rows_one, rows_two):
    shapes = [(share, rows_one), (share, rows_two)] + [(1, share)] * 4
    return call(
        finish_body,
        (got, back_one_sums, back_two_sums),
        [like(s, F32) for s in shapes],
    )


def exchange(blocks):
    return lax.all_to_all(blocks, AXES, 0, 0, tiled=True)


def shards(
    features, clip_starts, kernel_one, kernel_two, gain_one, shift_one, gain_two, shift_two, cotangent
):
    frames = features.shape[0]
    copies = lax.axis_size(AXES)
    row_count = lax.axis_size("row")
    count = float(frames * MEL * copies)
    rows_one, rows_two = kernel_one.shape[0], kernel_two.shape[0]
    share = kernel_one.shape[1]
    vectors = [v.reshape(1, share) for v in (gain_one, shift_one, gain_two, shift_two)]
    clips = clip_starts.reshape(1, -1)
    weights, up, down = setup(kernel_one.T, kernel_two.T, vectors, features, cotangent, copies)
    ends = copies - 1
    up = lax.ppermute(up, AXES, [(i, i + 1) for i in range(ends)])
    down = lax.ppermute(down, AXES, [(i + 1, i) for i in range(ends)])
    weights = exchange(weights)
    pre_one, stats, taps_x, masks, k1, k2, vec, weight = conv_one(
        features, up, down, clips, weights, row_count
    )
    stats = exchange(stats)
    pre_two, stats, taps_a, sums_one, weight_back = conv_two(
        pre_one, stats, vec, masks, k2, weight, count
    )
    stats = exchange(stats)
    block_out, lift, stats, sums_two = norm_two(pre_two, stats, vec, cotangent, up, down, count)
    stats = exchange(stats)
    lift, two, stats, back_two_sums = back_two(
        lift, pre_two, sums_two, stats, vec, masks, weight_back, pre_one, sums_one, taps_a, count
    )
    stats = exchange(stats)
    stored, blocks, back_one_sums = kernel_grads(
        lift, pre_one, sums_one, stats, vec, masks, taps_x, two, row_count, count
    )
    blocks = exchange(blocks)
    grad_features = features_grad(stored, k1)
    own_one, own_two, ga, sa, gb, sb = finish(
        blocks, back_one_sums, back_two_sums, share, rows_one, rows_two
    )
    return (
        block_out,
        grad_features,
        own_one.T,
        own_two.T,
        ga.reshape(share),
        sa.reshape(share),
        gb.reshape(share),
        sb.reshape(share),
    )


def solution(mesh):
    placed = (
        P(AXES, None), P(), P("row", "grp"), P("row", "grp"),
        P("grp"), P("grp"), P("grp"), P("grp"), P(AXES, None),
    )
    return jax.shard_map(
        shards,
        mesh=mesh,
        in_specs=placed,
        out_specs=(
            P(AXES, None), P(AXES, None), P("row", "grp"), P("row", "grp"),
            P("grp"), P("grp"), P("grp"), P("grp"),
        ),
        check_vma=False,
    )
```

profile of v0, /device:TPU:0, one launch (start us, length us, event | category | flops | bytes accessed | tf_op | source)
XLA Modules:
  0.0 113.6 jit_solution(2005731315821821986)
XLA Ops:
  0.6 0.0 copy-start
  0.6 0.0 copy-start.2
  0.7 2.1 %shard_map.152 = (bf16[32,56,128]{2,1,0:T(8,128)(2,1)}, bf16[8,2048]{1,0:T(8,128)(2,1)}, bf16[8,2048]{1,0:T(8,128)(2,1)}) custom-call(bf16[32,72]{1,0:T(8,128)(2,1)} %bitcast.15, bf16[32,144]{1,0:T(8,128)(2,1)} %bitcast.14, bf16[1,32]{1,0:T(2,128)(2,1)} %bitcast.16, bf16[1,32]{1,0:T(2,128)(2,1)} %bitcast.17, bf16[1,32]{1,0:T(2,128)(2,1)} %bitcast.18, ...), custom_call_target="tpu_custom_call" | custom-call | flops 5000000000 | tf_op jit(solution)/shard_map/pallas_call | solution.py:33
  2.8 7.3 %all-to-all-start = ((bf16[32,56,128]{2,1,0:T(8,128)(2,1)}), bf16[32,56,128]{2,1,0:T(8,128)(2,1)S(1)}, u32[]{:S(2)}, u32[]{:S(2)}) async-start(bf16[32,56,128]{2,1,0:T(8,128)(2,1)} %get-tuple-element.43), calls=%async_computation | async-start | bytes 917504 | tf_op jit(solution)/shard_map/all_to_all | solution.py:890
  10.1 3.7 %collective-permute-start = (bf16[8,2048]{1,0:T(8,128)(2,1)}, bf16[8,2048]{1,0:T(8,128)(2,1)S(1)}, u32[]{:S(2)}, u32[]{:S(2)}) collective-permute-start(bf16[8,2048]{1,0:T(8,128)(2,1)} %get-tuple-element.41), channel_id=1, source_target_pairs={{0,1},{1,2},{2,3},{3,4},{4,5},{5,6},{6,7},{7,8},{8,9},{9,10},{10,1... | collective-permute-start | bytes 98312 | tf_op jit(solution)/shard_map/ppermute | solution.py:906
  13.8 1.3 %collective-permute-start.1 = (bf16[8,2048]{1,0:T(8,128)(2,1)}, bf16[8,2048]{1,0:T(8,128)(2,1)S(1)}, u32[]{:S(2)}, u32[]{:S(2)}) collective-permute-start(bf16[8,2048]{1,0:T(8,128)(2,1)} %get-tuple-element.42), channel_id=1, source_target_pairs={{1,0},{2,1},{3,2},{4,3},{5,4},{6,5},{7,6},{8,7},{9,8},{10,9},{11,1... | collective-permute-start | bytes 98312 | tf_op jit(solution)/shard_map/ppermute | solution.py:907
  15.1 1.5 %collective-permute-done.refs_1_.refs_4_ = bf16[8,2048]{1,0:T(8,128)(2,1)S(1)} collective-permute-done((bf16[8,2048]{1,0:T(8,128)(2,1)}, bf16[8,2048]{1,0:T(8,128)(2,1)S(1)}, u32[]{:S(2)}, u32[]{:S(2)}) %collective-permute-start) | collective-permute-done | bytes 32800 | tf_op jit(solution)/shard_map/ppermute | solution.py:906
  16.6 3.3 %collective-permute-done.1.refs_2_.refs_5_ = bf16[8,2048]{1,0:T(8,128)(2,1)S(1)} collective-permute-done((bf16[8,2048]{1,0:T(8,128)(2,1)}, bf16[8,2048]{1,0:T(8,128)(2,1)S(1)}, u32[]{:S(2)}, u32[]{:S(2)}) %collective-permute-start.1) | collective-permute-done | bytes 32800 | tf_op jit(solution)/shard_map/ppermute | solution.py:907
  19.9 5.5 %all-to-all-done.refs_4_ = bf16[32,56,128]{2,1,0:T(8,128)(2,1)S(1)} async-done(((bf16[32,56,128]{2,1,0:T(8,128)(2,1)}), bf16[32,56,128]{2,1,0:T(8,128)(2,1)S(1)}, u32[]{:S(2)}, u32[]{:S(2)}) %all-to-all-start) | async-done | bytes 458784 | tf_op jit(solution)/shard_map/all_to_all | solution.py:890
  25.4 0.0 copy-done
  25.4 0.0 copy-done.2
  25.4 5.2 %shard_map.153 = (f32[32,208,256]{2,1,0:T(8,128)S(1)}, f32[32,2,128]{2,1,0:T(2,128)S(1)}, bf16[18,208,512]{2,1,0:T(8,128)(2,1)S(1)}, f32[2,208,128]{2,1,0:T(8,12...) custom-call(bf16[384,2048]{1,0:T(8,128)(2,1)S(1)} %copy-done, ...), custom_call_target="tpu_custom_call" | custom-call | flops 5000000000 | tf_op jit(solution)/shard_map/pallas_call | solution.py:33
  30.6 9.5 %all_to_all.30.refs_1_ = f32[32,2,128]{2,1,0:T(2,128)S(1)} all-to-all(f32[32,2,128]{2,1,0:T(2,128)S(1)} %get-tuple-element.45), channel_id=1, replica_groups=mesh['grp'=4,'row'=8] {'grp','row'}, dimensions={0} | all-to-all | bytes 65536 | tf_op jit(solution)/shard_map/all_to_all | solution.py:890
  40.0 6.7 %shard_map.154 = (f32[32,208,256]{2,1,0:T(8,128)S(1)}, f32[32,2,128]{2,1,0:T(2,128)S(1)}, bf16[34,208,512]{2,1,0:T(8,128)(2,1)S(1)}, f32[2,128]{1,0:T(2,128)S(1)}, bf16[1536,256]{1,0:T(8,128)(2,1)S(1)}) custom-call(f32[32,208,256]{2,1,0:T(8,128)S(1)} %get-tuple-element.44.refs_0_.refs_7_.refs_1_, f32[32,2,128]{2,1,0:T(2,128)S(1)} %all_to_all.30.refs_1_, ...), custom_call_target="tpu_custom_call" | custom-call | flops 5000000000 | tf_op jit(solution)/shard_map/pallas_call | solution.py:33
  46.7 8.9 %all_to_all.31.refs_1_ = f32[32,2,128]{2,1,0:T(2,128)S(1)} all-to-all(f32[32,2,128]{2,1,0:T(2,128)S(1)} %get-tuple-element.51), channel_id=1, replica_groups=mesh['grp'=4,'row'=8] {'grp','row'}, dimensions={0} | all-to-all | bytes 65536 | tf_op jit(solution)/shard_map/all_to_all | solution.py:890
  55.6 4.0 %shard_map.155 = (bf16[192,2048]{1,0:T(8,128)(2,1)}, f32[32,208,256]{2,1,0:T(8,128)S(1)}, f32[32,2,128]{2,1,0:T(2,128)S(1)}, f32[2,128]{1,0:T(2,128)S(1)}) custom-call(f32[32,208,256]{2,1,0:T(8,128)S(1)} %get-tuple-element.50.refs_0_.refs_1_, f32[32,2,128]{2,1,0:T(2,128)S(1)} %all_to_all.31.refs_1_, f32[4,128]{1,0:T(4,128)S(1)} %get-tuple-element.46.refs_2_.refs_4_, ...), custom_call_target="tpu_custom_call" | custom-call | flops 5000000000 | tf_op jit(solution)/shard_map/pallas_call | solution.py:33
  59.6 8.9 %all_to_all.32.refs_3_ = f32[32,2,128]{2,1,0:T(2,128)S(1)} all-to-all(f32[32,2,128]{2,1,0:T(2,128)S(1)} %get-tuple-element.55), channel_id=1, replica_groups=mesh['grp'=4,'row'=8] {'grp','row'}, dimensions={0} | all-to-all | bytes 65536 | tf_op jit(solution)/shard_map/all_to_all | solution.py:890
  68.4 12.9 %shard_map.156 = (f32[32,208,256]{2,1,0:T(8,128)S(1)}, f32[128,1152]{1,0:T(8,128)S(1)}, f32[32,2,128]{2,1,0:T(2,128)S(1)}, f32[2,128]{1,0:T(2,128)S(1)}) custom-call(f32[32,208,256]{2,1,0:T(8,128)S(1)} %get-tuple-element.53.refs_0_, f32[32,208,256]{2,1,0:T(8,128)S(1)} %get-tuple-element.50.refs_0_.refs_1_, ...), custom_call_target="tpu_custom_call", output_to_operand_aliasing={{0}: (0, {})} | custom-call | flops 5000000000 | tf_op jit(solution)/shard_map/pallas_call | solution.py:33
  81.3 8.9 %all_to_all.33.refs_3_ = f32[32,2,128]{2,1,0:T(2,128)S(1)} all-to-all(f32[32,2,128]{2,1,0:T(2,128)S(1)} %get-tuple-element.60), channel_id=1, replica_groups=mesh['grp'=4,'row'=8] {'grp','row'}, dimensions={0} | all-to-all | bytes 65536 | tf_op jit(solution)/shard_map/all_to_all | solution.py:890
  90.2 5.0 %shard_map.157 = (bf16[640,208,256]{2,1,0:T(8,128)(2,1)}, bf16[32,56,128]{2,1,0:T(8,128)(2,1)}, f32[2,128]{1,0:T(2,128)S(1)}) custom-call(f32[32,208,256]{2,1,0:T(8,128)S(1)} %get-tuple-element.59.refs_0_, f32[32,208,256]{2,1,0:T(8,128)S(1)} %get-tuple-element.44.refs_0_.refs_7_.refs_1_, f32[2,128]{1,0:T(2,128)S(1)} %get-tuple-element.57.refs_8_.refs_2_, ...), custom_call_target="tpu_custom_call" | custom-call | flops 5000000000 | tf_op jit(solution)/shard_map/pallas_call | solution.py:33
  95.2 2.6 %all-to-all-start.5 = ((bf16[32,56,128]{2,1,0:T(8,128)(2,1)}), bf16[32,56,128]{2,1,0:T(8,128)(2,1)S(1)}, u32[]{:S(2)}, u32[]{:S(2)}) async-start(bf16[32,56,128]{2,1,0:T(8,128)(2,1)} %get-tuple-element.65), calls=%async_computation.5 | async-start | bytes 917504 | tf_op jit(solution)/shard_map/all_to_all | solution.py:890
  97.8 10.3 %shard_map.158 = f32[384,2048]{1,0:T(8,128)} custom-call(bf16[640,208,256]{2,1,0:T(8,128)(2,1)} %get-tuple-element.63.stored, bf16[576,128]{1,0:T(8,128)(2,1)S(1)} %get-tuple-element.64.k1), custom_call_target="tpu_custom_call" | custom-call | flops 5000000000 | tf_op jit(solution)/shard_map/pallas_call | solution.py:33
  108.1 4.6 %all-to-all-done.5.got = bf16[32,56,128]{2,1,0:T(8,128)(2,1)S(1)} async-done(((bf16[32,56,128]{2,1,0:T(8,128)(2,1)}), bf16[32,56,128]{2,1,0:T(8,128)(2,1)S(1)}, u32[]{:S(2)}, u32[]{:S(2)}) %all-to-all-start.5) | async-done | bytes 458784 | tf_op jit(solution)/shard_map/all_to_all | solution.py:890
  112.8 0.8 shard_map.159
  (2 shorter events, 0.0 us)
Async XLA Ops:
  0.6 24.8 %copy-start = (bf16[384,2048]{1,0:T(8,128)(2,1)S(1)}, bf16[384,2048]{1,0:T(8,128)(2,1)}, u32[]{:S(2)}) copy-start(bf16[384,2048]{1,0:T(8,128)(2,1)} %refs_0_.1) | copy-start | bytes 4718596
  0.6 24.8 %copy-start.2 = (s32[64]{0:T(128)S(1)}, s32[64]{0:T(128)}, u32[]{:S(2)}) copy-start(s32[64]{0:T(128)} %param.10) | copy-start | bytes 772
  2.8 22.6 %all-to-all-start = ((bf16[32,56,128]{2,1,0:T(8,128)(2,1)}), bf16[32,56,128]{2,1,0:T(8,128)(2,1)S(1)}, u32[]{:S(2)}, u32[]{:S(2)}) async-start(bf16[32,56,128]{2,1,0:T(8,128)(2,1)} %get-tuple-element.43), calls=%async_computation | async-start | bytes 917504 | tf_op jit(solution)/shard_map/all_to_all | solution.py:890
  10.1 6.5 %collective-permute-start = (bf16[8,2048]{1,0:T(8,128)(2,1)}, bf16[8,2048]{1,0:T(8,128)(2,1)S(1)}, u32[]{:S(2)}, u32[]{:S(2)}) collective-permute-start(bf16[8,2048]{1,0:T(8,128)(2,1)} %get-tuple-element.41), channel_id=1, source_target_pairs={{0,1},{1,2},{2,3},{3,4},{4,5},{5,6},{6,7},{7,8},{8,9},{9,10},{10,1... | collective-permute-start | bytes 98312 | tf_op jit(solution)/shard_map/ppermute | solution.py:906
  13.8 6.1 %collective-permute-start.1 = (bf16[8,2048]{1,0:T(8,128)(2,1)}, bf16[8,2048]{1,0:T(8,128)(2,1)S(1)}, u32[]{:S(2)}, u32[]{:S(2)}) collective-permute-start(bf16[8,2048]{1,0:T(8,128)(2,1)} %get-tuple-element.42), channel_id=1, source_target_pairs={{1,0},{2,1},{3,2},{4,3},{5,4},{6,5},{7,6},{8,7},{9,8},{10,9},{11,1... | collective-permute-start | bytes 98312 | tf_op jit(solution)/shard_map/ppermute | solution.py:907
  40.0 15.6 %copy-start.1 = (bf16[192,2048]{1,0:T(8,128)(2,1)S(1)}, bf16[192,2048]{1,0:T(8,128)(2,1)}, u32[]{:S(2)}) copy-start(bf16[192,2048]{1,0:T(8,128)(2,1)} %refs_3_.1) | copy-start | bytes 2359300
  95.2 17.6 %all-to-all-start.5 = ((bf16[32,56,128]{2,1,0:T(8,128)(2,1)}), bf16[32,56,128]{2,1,0:T(8,128)(2,1)S(1)}, u32[]{:S(2)}, u32[]{:S(2)}) async-start(bf16[32,56,128]{2,1,0:T(8,128)(2,1)} %get-tuple-element.65), calls=%async_computation.5 | async-start | bytes 917504 | tf_op jit(solution)/shard_map/all_to_all | solution.py:890
where the time goes:
time: 114 us
  Pallas kernels  46.9 us (41%)
  blocking collectives  36.1 us (32%)
  waiting for transfers between devices  15 us (13%)
  starting transfers between devices  14.9 us (13%)
    pallas_call x8, Pallas kernels, call(): pl.pallas_call(body, in_specs=in_specs or [VMEM] * len(args), out_specs=o...  46.9 us
    all_to_all x4, blocking collectives, exchange(): return lax.all_to_all(blocks, AXES, 0, 0, tiled=True)  36.1 us
    all_to_all x2, waiting for transfers between devices, exchange(): return lax.all_to_all(blocks, AXES, 0, 0, tiled=True)  10.1 us
    all_to_all x2, starting transfers between devices, exchange(): return lax.all_to_all(blocks, AXES, 0, 0, tiled=True)  9.91 us
    ppermute x1, starting transfers between devices, shards(): up = lax.ppermute(up, AXES, [(i, i + 1) for i in range(ends)])  3.67 us
    ppermute x1, waiting for transfers between devices, shards(): down = lax.ppermute(down, AXES, [(i + 1, i) for i in range(ends)])  3.31 us
  transfers between devices with their start and end apart: 4, of which 4 were waited for; matrix products, arithmetic and copies ran while one was open for 0% of the time, Pallas kernels for 9%

commit v1 on v0

--- a/solution.py
+++ b/solution.py
@@ -60,13 +60,16 @@
         return jnp.concatenate(
             [block[:, at : at + LANES] for at in range(0, block.shape[1], LANES)], axis=0
         )
-    rest = block[:, LANES:]
-    room = 2 * LANES - wide
+    return jnp.concatenate([block[:, :LANES], pack_rest(block[:, LANES:])], axis=0)
+
+
+def pack_rest(rest):
+    room = LANES - rest.shape[1]
     tail = jnp.concatenate(
         [rest[24:32], jnp.zeros((8, 3 * room - rest.shape[1]), F32)], axis=1
     )
     tail = jnp.concatenate([tail[:, k * room : (k + 1) * room] for k in range(3)], axis=0)
-    return jnp.concatenate([block[:, :LANES], jnp.concatenate([rest[0:24], tail], axis=1)], axis=0)
+    return jnp.concatenate([rest[0:24], tail], axis=1)
 
 
 def unpack(block, share, wide):
@@ -622,16 +625,25 @@
 
     def correlate(k):
         here = range(k * wide_mels, (k + 1) * wide_mels)
-        turned[...] = stack(taps, here, half, slice(128, 384)).T
-        for d in range(3):
-            first = here[0] + d
-            near = taps_a[first : first + wide_mels, 0:half].reshape(wide_mels * half, WIDE)
-            total = jnp.dot(turned[...], near, preferred_element_type=F32)
-            lanes = slice(d * WIDE, (d + 1) * WIDE)
-            if k == 0:
-                acc_two[:, lanes] = total
+        flat = wide_mels * half
+        chosen = stack(taps, here, half, slice(128, 384)).T
+        for p in range(2):
+            turned[:, p * flat : (p + 1) * flat] = chosen[p * C_MID : (p + 1) * C_MID]
+        for p in range(2):
+            near = []
+            for d in range(3):
+                first = here[0] + d
+                lanes = slice(p * LANES, p * LANES + 3 * LANES)
+                near.append(taps_a[first : first + wide_mels, 0:half, lanes].reshape(flat, 3 * LANES))
+            total = jnp.dot(
+                turned[:, p * flat : (p + 1) * flat],
+                jnp.concatenate(near, axis=1),
+                preferred_element_type=F32,
+            )
+            if k == 0 and p == 0:
+                acc_two[...] = total
             else:
-                acc_two[:, lanes] += total
+                acc_two[...] += total
 
     for k in range(MEL // mels + 1):
         for m in range(k * mels, (k + 1) * mels):
@@ -645,11 +657,9 @@
     spread(plain, normed_sum(fold(acc[1]), plain, vec[0:1], vec[1:2]), back_out)
     for t in range(3):
         for d in range(3):
-            at = d * WIDE + t * 128
+            at = (3 * d + t) * 128
             to = (3 * t + d) * 128
-            two[:, to : to + 128] = (
-                acc_two[0:C_MID, at : at + 128] + acc_two[C_MID:BOTH, at + 128 : at + 256]
-            )
+            two[:, to : to + 128] = acc_two[:, at : at + 128]
 
 
 def back_two(lift, pre_two, sums_two, back_stats, vec, masks, weight, pre_one, sums_one, taps_a, count):
@@ -666,8 +676,8 @@
         ],
         [
             pltpu.VMEM((2, 8, BOTH), F32),
-            pltpu.VMEM((BOTH, 3 * WIDE), F32),
-            pltpu.VMEM((BOTH, 4 * (rows - TAIL)), BF16),
+            pltpu.VMEM((C_MID, 9 * C_MID), F32),
+            pltpu.VMEM((C_MID, 8 * (rows - TAIL)), BF16),
             *side_scratch(rows),
             *ring_scratch(17, rows),
         ],
@@ -676,18 +686,37 @@
     )
 
 
-def scatter_blocks(out, parts, row_count):
-    copies = out.shape[0]
+def scatter_blocks(out, tops, two, one, row_count):
+    copies, block_rows = out.shape[0:2]
     grps = copies // row_count
     share = C_MID // grps
-    turned = [part.T for part in parts]
-    sizes = [part.shape[1] // row_count for part in parts]
-    for r in range(row_count):
-        rows = [t[n * r : n * (r + 1)] for t, n in zip(turned, sizes)]
-        back = jnp.concatenate(rows, axis=0).T
-        for g in range(grps):
-            block = back[share * g : share * (g + 1)]
-            out[g * row_count + r] = pack(block, out.shape[1]).astype(BF16)
+    size_two = 9 * C_MID // row_count
+    size_one = 9 * C_IN // row_count
+    ahead = LANES if block_rows == share + 24 and size_two >= LANES else 0
+
+    def first():
+        turned = two[...].T
+        for r in range(row_count if ahead else 0):
+            tops[r] = turned[size_two * r : size_two * r + ahead].T
+
+    def second():
+        turned = two[...].T
+        turned_one = one().T
+        for r in range(row_count):
+            rows = [
+                turned[size_two * r + ahead : size_two * (r + 1)],
+                turned_one[size_one * r : size_one * (r + 1)],
+            ]
+            back = jnp.concatenate(rows, axis=0).T
+            for g in range(grps):
+                here = slice(share * g, share * (g + 1))
+                if ahead:
+                    block = jnp.concatenate([tops[r, here], pack_rest(back[here])], axis=0)
+                else:
+                    block = pack(back[here], block_rows)
+                out[g * row_count + r] = block.astype(BF16)
+
+    return first, second
 
 
 def kernel_one_step(taps_x, grads, acc, k, pairs):
@@ -718,7 +747,7 @@
 
 
 def grads_body(count, row_count, lift, pre_one, sums_one, back_stats, vec, masks, taps_x, two,
-               stored, blocks, sums_out, acc_one, grads, low_masks, sems):
+               stored, blocks, sums_out, acc_one, grads, low_masks, tops, sems):
     back = stat_sums(back_stats)
     sums_out[...] = back
     a, b, c = grad_terms(sums_one[...], back, vec[0:1], count)
@@ -733,10 +762,15 @@
             span = slice(r, r + TILE)
             grads[m, span] = (lift[m, span] * a + (pre_one[m, span] * b + c)).astype(BF16)
 
+    scatter_ahead, scatter_rest = scatter_blocks(
+        blocks, tops, two, lambda: kernel_one_sums(acc_one), row_count
+    )
     pairs = 2
     mels = 2 * pairs
     steps = MEL // mels
     for k in range(steps + 1):
+        if k == 2:
+            scatter_ahead()
         if k < steps:
             for m in range(mels * k, mels * (k + 1)):
                 lower(m)
@@ -745,7 +779,7 @@
             copies[-1].start()
         if k > 0:
             kernel_one_step(taps_x, grads, acc_one, k - 1, pairs)
-    scatter_blocks(blocks, [kernel_one_sums(acc_one), two[...]], row_count)
+    scatter_rest()
     for copy in copies:
         copy.wait()
 
@@ -767,6 +801,7 @@
             pltpu.VMEM((BOTH, 3 * BOTH), F32),
             pltpu.VMEM((MEL, rows, BOTH), BF16),
             pltpu.VMEM((rows, BOTH), BF16),
+            pltpu.VMEM((row_count, C_MID, LANES), F32),
             pltpu.SemaphoreType.DMA((9,)),
         ],
         out_specs=[HBM, VMEM, VMEM],
@@ -857,12 +892,12 @@
 
 
 def finish_body(got, back_one_sums, back_two_sums, own_one, own_two, ga, sa, gb, sb):
-    size = own_one.shape[1]
-    share = own_one.shape[0]
+    size = own_two.shape[1]
+    share = own_two.shape[0]
     total = jnp.sum(got[...].astype(F32), axis=0)
-    total = unpack(total, share, size + own_two.shape[1])
-    own_one[...] = total[:, 0:size]
-    own_two[...] = total[:, size:]
+    total = unpack(total, share, size + own_one.shape[1])
+    own_two[...] = total[:, 0:size]
+    own_one[...] = total[:, size:]
     lane = lax.broadcasted_iota(jnp.int32, (share, C_MID), 1)
     row = lax.broadcasted_iota(jnp.int32, (share, C_MID), 0)
     chosen = lane == lax.axis_index("grp") * share + row

time: 114 us -> 113 us (level)
  no operation moved by 1% of the time
where the time goes in v1:
time: 113 us
  Pallas kernels  46.1 us (41%)
  blocking collectives  36.1 us (32%)
  waiting for transfers between devices  15 us (13%)
  starting transfers between devices  14.9 us (13%)
    pallas_call x8, Pallas kernels, call(): pl.pallas_call(body, in_specs=in_specs or [VMEM] * len(args), out_specs=o...  46.1 us
    all_to_all x4, blocking collectives, exchange(): return lax.all_to_all(blocks, AXES, 0, 0, tiled=True)  36.1 us
    all_to_all x2, waiting for transfers between devices, exchange(): return lax.all_to_all(blocks, AXES, 0, 0, tiled=True)  10.1 us
    all_to_all x2, starting transfers between devices, exchange(): return lax.all_to_all(blocks, AXES, 0, 0, tiled=True)  9.91 us
    ppermute x1, starting transfers between devices, shards(): up = lax.ppermute(up, AXES, [(i, i + 1) for i in range(ends)])  3.67 us
    ppermute x1, waiting for transfers between devices, shards(): down = lax.ppermute(down, AXES, [(i + 1, i) for i in range(ends)])  3.31 us
  transfers between devices with their start and end apart: 4, of which 4 were waited for; matrix products, arithmetic and copies ran while one was open for 0% of the time, Pallas kernels for 9%

profile of v1, /device:TPU:0, one launch (start us, length us, event | category | flops | bytes accessed | tf_op | source)
XLA Modules:
  0.0 112.8 jit_solution(8894869702900589965)
XLA Ops:
  0.6 0.0 copy-start
  0.6 0.0 copy-start.2
  0.7 2.1 %shard_map.152 = (bf16[32,56,128]{2,1,0:T(8,128)(2,1)}, bf16[8,2048]{1,0:T(8,128)(2,1)}, bf16[8,2048]{1,0:T(8,128)(2,1)}) custom-call(bf16[32,72]{1,0:T(8,128)(2,1)} %bitcast.15, bf16[32,144]{1,0:T(8,128)(2,1)} %bitcast.14, bf16[1,32]{1,0:T(2,128)(2,1)} %bitcast.16, bf16[1,32]{1,0:T(2,128)(2,1)} %bitcast.17, bf16[1,32]{1,0:T(2,128)(2,1)} %bitcast.18, ...), custom_call_target="tpu_custom_call" | custom-call | flops 5000000000 | tf_op jit(solution)/shard_map/pallas_call | solution.py:33
  2.8 7.3 %all-to-all-start = ((bf16[32,56,128]{2,1,0:T(8,128)(2,1)}), bf16[32,56,128]{2,1,0:T(8,128)(2,1)S(1)}, u32[]{:S(2)}, u32[]{:S(2)}) async-start(bf16[32,56,128]{2,1,0:T(8,128)(2,1)} %get-tuple-element.43), calls=%async_computation | async-start | bytes 917504 | tf_op jit(solution)/shard_map/all_to_all | solution.py:925
  10.1 3.7 %collective-permute-start = (bf16[8,2048]{1,0:T(8,128)(2,1)}, bf16[8,2048]{1,0:T(8,128)(2,1)S(1)}, u32[]{:S(2)}, u32[]{:S(2)}) collective-permute-start(bf16[8,2048]{1,0:T(8,128)(2,1)} %get-tuple-element.41), channel_id=1, source_target_pairs={{0,1},{1,2},{2,3},{3,4},{4,5},{5,6},{6,7},{7,8},{8,9},{9,10},{10,1... | collective-permute-start | bytes 98312 | tf_op jit(solution)/shard_map/ppermute | solution.py:941
  13.8 1.3 %collective-permute-start.1 = (bf16[8,2048]{1,0:T(8,128)(2,1)}, bf16[8,2048]{1,0:T(8,128)(2,1)S(1)}, u32[]{:S(2)}, u32[]{:S(2)}) collective-permute-start(bf16[8,2048]{1,0:T(8,128)(2,1)} %get-tuple-element.42), channel_id=1, source_target_pairs={{1,0},{2,1},{3,2},{4,3},{5,4},{6,5},{7,6},{8,7},{9,8},{10,9},{11,1... | collective-permute-start | bytes 98312 | tf_op jit(solution)/shard_map/ppermute | solution.py:942
  15.1 1.5 %collective-permute-done.refs_1_.refs_4_ = bf16[8,2048]{1,0:T(8,128)(2,1)S(1)} collective-permute-done((bf16[8,2048]{1,0:T(8,128)(2,1)}, bf16[8,2048]{1,0:T(8,128)(2,1)S(1)}, u32[]{:S(2)}, u32[]{:S(2)}) %collective-permute-start) | collective-permute-done | bytes 32800 | tf_op jit(solution)/shard_map/ppermute | solution.py:941
  16.6 3.3 %collective-permute-done.1.refs_2_.refs_5_ = bf16[8,2048]{1,0:T(8,128)(2,1)S(1)} collective-permute-done((bf16[8,2048]{1,0:T(8,128)(2,1)}, bf16[8,2048]{1,0:T(8,128)(2,1)S(1)}, u32[]{:S(2)}, u32[]{:S(2)}) %collective-permute-start.1) | collective-permute-done | bytes 32800 | tf_op jit(solution)/shard_map/ppermute | solution.py:942
  19.9 5.5 %all-to-all-done.refs_4_ = bf16[32,56,128]{2,1,0:T(8,128)(2,1)S(1)} async-done(((bf16[32,56,128]{2,1,0:T(8,128)(2,1)}), bf16[32,56,128]{2,1,0:T(8,128)(2,1)S(1)}, u32[]{:S(2)}, u32[]{:S(2)}) %all-to-all-start) | async-done | bytes 458784 | tf_op jit(solution)/shard_map/all_to_all | solution.py:925
  25.4 0.0 copy-done
  25.4 0.0 copy-done.2
  25.4 5.2 %shard_map.153 = (f32[32,208,256]{2,1,0:T(8,128)S(1)}, f32[32,2,128]{2,1,0:T(2,128)S(1)}, bf16[18,208,512]{2,1,0:T(8,128)(2,1)S(1)}, f32[2,208,128]{2,1,0:T(8,12...) custom-call(bf16[384,2048]{1,0:T(8,128)(2,1)S(1)} %copy-done, ...), custom_call_target="tpu_custom_call" | custom-call | flops 5000000000 | tf_op jit(solution)/shard_map/pallas_call | solution.py:33
  30.6 9.5 %all_to_all.30.refs_1_ = f32[32,2,128]{2,1,0:T(2,128)S(1)} all-to-all(f32[32,2,128]{2,1,0:T(2,128)S(1)} %get-tuple-element.45), channel_id=1, replica_groups=mesh['grp'=4,'row'=8] {'grp','row'}, dimensions={0} | all-to-all | bytes 65536 | tf_op jit(solution)/shard_map/all_to_all | solution.py:925
  40.0 6.7 %shard_map.154 = (f32[32,208,256]{2,1,0:T(8,128)S(1)}, f32[32,2,128]{2,1,0:T(2,128)S(1)}, bf16[34,208,512]{2,1,0:T(8,128)(2,1)S(1)}, f32[2,128]{1,0:T(2,128)S(1)}, bf16[1536,256]{1,0:T(8,128)(2,1)S(1)}) custom-call(f32[32,208,256]{2,1,0:T(8,128)S(1)} %get-tuple-element.44.refs_0_.refs_7_.refs_1_, f32[32,2,128]{2,1,0:T(2,128)S(1)} %all_to_all.30.refs_1_, ...), custom_call_target="tpu_custom_call" | custom-call | flops 5000000000 | tf_op jit(solution)/shard_map/pallas_call | solution.py:33
  46.7 8.9 %all_to_all.31.refs_1_ = f32[32,2,128]{2,1,0:T(2,128)S(1)} all-to-all(f32[32,2,128]{2,1,0:T(2,128)S(1)} %get-tuple-element.51), channel_id=1, replica_groups=mesh['grp'=4,'row'=8] {'grp','row'}, dimensions={0} | all-to-all | bytes 65536 | tf_op jit(solution)/shard_map/all_to_all | solution.py:925
  55.6 4.0 %shard_map.155 = (bf16[192,2048]{1,0:T(8,128)(2,1)}, f32[32,208,256]{2,1,0:T(8,128)S(1)}, f32[32,2,128]{2,1,0:T(2,128)S(1)}, f32[2,128]{1,0:T(2,128)S(1)}) custom-call(f32[32,208,256]{2,1,0:T(8,128)S(1)} %get-tuple-element.50.refs_0_.refs_1_, f32[32,2,128]{2,1,0:T(2,128)S(1)} %all_to_all.31.refs_1_, f32[4,128]{1,0:T(4,128)S(1)} %get-tuple-element.46.refs_2_.refs_4_, ...), custom_call_target="tpu_custom_call" | custom-call | flops 5000000000 | tf_op jit(solution)/shard_map/pallas_call | solution.py:33
  59.6 8.9 %all_to_all.32.refs_3_ = f32[32,2,128]{2,1,0:T(2,128)S(1)} all-to-all(f32[32,2,128]{2,1,0:T(2,128)S(1)} %get-tuple-element.55), channel_id=1, replica_groups=mesh['grp'=4,'row'=8] {'grp','row'}, dimensions={0} | all-to-all | bytes 65536 | tf_op jit(solution)/shard_map/all_to_all | solution.py:925
  68.4 12.3 %shard_map.156 = (f32[32,208,256]{2,1,0:T(8,128)S(1)}, f32[128,1152]{1,0:T(8,128)S(1)}, f32[32,2,128]{2,1,0:T(2,128)S(1)}, f32[2,128]{1,0:T(2,128)S(1)}) custom-call(f32[32,208,256]{2,1,0:T(8,128)S(1)} %get-tuple-element.53.refs_0_, f32[32,208,256]{2,1,0:T(8,128)S(1)} %get-tuple-element.50.refs_0_.refs_1_, ...), custom_call_target="tpu_custom_call", output_to_operand_aliasing={{0}: (0, {})} | custom-call | flops 5000000000 | tf_op jit(solution)/shard_map/pallas_call | solution.py:33
  80.7 8.9 %all_to_all.33.refs_3_ = f32[32,2,128]{2,1,0:T(2,128)S(1)} all-to-all(f32[32,2,128]{2,1,0:T(2,128)S(1)} %get-tuple-element.60), channel_id=1, replica_groups=mesh['grp'=4,'row'=8] {'grp','row'}, dimensions={0} | all-to-all | bytes 65536 | tf_op jit(solution)/shard_map/all_to_all | solution.py:925
  89.6 4.8 %shard_map.157 = (bf16[640,208,256]{2,1,0:T(8,128)(2,1)}, bf16[32,56,128]{2,1,0:T(8,128)(2,1)}, f32[2,128]{1,0:T(2,128)S(1)}) custom-call(f32[32,208,256]{2,1,0:T(8,128)S(1)} %get-tuple-element.59.refs_0_, f32[32,208,256]{2,1,0:T(8,128)S(1)} %get-tuple-element.44.refs_0_.refs_7_.refs_1_, f32[2,128]{1,0:T(2,128)S(1)} %get-tuple-element.57.refs_8_.refs_2_, ...), custom_call_target="tpu_custom_call" | custom-call | flops 5000000000 | tf_op jit(solution)/shard_map/pallas_call | solution.py:33
  94.4 2.6 %all-to-all-start.5 = ((bf16[32,56,128]{2,1,0:T(8,128)(2,1)}), bf16[32,56,128]{2,1,0:T(8,128)(2,1)S(1)}, u32[]{:S(2)}, u32[]{:S(2)}) async-start(bf16[32,56,128]{2,1,0:T(8,128)(2,1)} %get-tuple-element.65), calls=%async_computation.5 | async-start | bytes 917504 | tf_op jit(solution)/shard_map/all_to_all | solution.py:925
  97.0 10.3 %shard_map.158 = f32[384,2048]{1,0:T(8,128)} custom-call(bf16[640,208,256]{2,1,0:T(8,128)(2,1)} %get-tuple-element.63.stored, bf16[576,128]{1,0:T(8,128)(2,1)S(1)} %get-tuple-element.64.k1), custom_call_target="tpu_custom_call" | custom-call | flops 5000000000 | tf_op jit(solution)/shard_map/pallas_call | solution.py:33
  107.3 4.6 %all-to-all-done.5.got = bf16[32,56,128]{2,1,0:T(8,128)(2,1)S(1)} async-done(((bf16[32,56,128]{2,1,0:T(8,128)(2,1)}), bf16[32,56,128]{2,1,0:T(8,128)(2,1)S(1)}, u32[]{:S(2)}, u32[]{:S(2)}) %all-to-all-start.5) | async-done | bytes 458784 | tf_op jit(solution)/shard_map/all_to_all | solution.py:925
  112.0 0.8 shard_map.159
  (2 shorter events, 0.0 us)
Async XLA Ops:
  0.6 24.8 %copy-start = (bf16[384,2048]{1,0:T(8,128)(2,1)S(1)}, bf16[384,2048]{1,0:T(8,128)(2,1)}, u32[]{:S(2)}) copy-start(bf16[384,2048]{1,0:T(8,128)(2,1)} %refs_0_.1) | copy-start | bytes 4718596
  0.6 24.8 %copy-start.2 = (s32[64]{0:T(128)S(1)}, s32[64]{0:T(128)}, u32[]{:S(2)}) copy-start(s32[64]{0:T(128)} %param.10) | copy-start | bytes 772
  2.8 22.6 %all-to-all-start = ((bf16[32,56,128]{2,1,0:T(8,128)(2,1)}), bf16[32,56,128]{2,1,0:T(8,128)(2,1)S(1)}, u32[]{:S(2)}, u32[]{:S(2)}) async-start(bf16[32,56,128]{2,1,0:T(8,128)(2,1)} %get-tuple-element.43), calls=%async_computation | async-start | bytes 917504 | tf_op jit(solution)/shard_map/all_to_all | solution.py:925
  10.1 6.5 %collective-permute-start = (bf16[8,2048]{1,0:T(8,128)(2,1)}, bf16[8,2048]{1,0:T(8,128)(2,1)S(1)}, u32[]{:S(2)}, u32[]{:S(2)}) collective-permute-start(bf16[8,2048]{1,0:T(8,128)(2,1)} %get-tuple-element.41), channel_id=1, source_target_pairs={{0,1},{1,2},{2,3},{3,4},{4,5},{5,6},{6,7},{7,8},{8,9},{9,10},{10,1... | collective-permute-start | bytes 98312 | tf_op jit(solution)/shard_map/ppermute | solution.py:941
  13.8 6.1 %collective-permute-start.1 = (bf16[8,2048]{1,0:T(8,128)(2,1)}, bf16[8,2048]{1,0:T(8,128)(2,1)S(1)}, u32[]{:S(2)}, u32[]{:S(2)}) collective-permute-start(bf16[8,2048]{1,0:T(8,128)(2,1)} %get-tuple-element.42), channel_id=1, source_target_pairs={{1,0},{2,1},{3,2},{4,3},{5,4},{6,5},{7,6},{8,7},{9,8},{10,9},{11,1... | collective-permute-start | bytes 98312 | tf_op jit(solution)/shard_map/ppermute | solution.py:942
  40.0 15.6 %copy-start.1 = (bf16[192,2048]{1,0:T(8,128)(2,1)S(1)}, bf16[192,2048]{1,0:T(8,128)(2,1)}, u32[]{:S(2)}) copy-start(bf16[192,2048]{1,0:T(8,128)(2,1)} %refs_3_.1) | copy-start | bytes 2359300
  94.4 17.6 %all-to-all-start.5 = ((bf16[32,56,128]{2,1,0:T(8,128)(2,1)}), bf16[32,56,128]{2,1,0:T(8,128)(2,1)S(1)}, u32[]{:S(2)}, u32[]{:S(2)}) async-start(bf16[32,56,128]{2,1,0:T(8,128)(2,1)} %get-tuple-element.65), calls=%async_computation.5 | async-start | bytes 917504 | tf_op jit(solution)/shard_map/all_to_all | solution.py:925

commit v2 on v1

--- a/solution.py
+++ b/solution.py
@@ -314,7 +314,7 @@
 
 
 def conv_one_body(row_count, features, up, down, clips_in, wg,
-                  pre, stats, taps, masks, k1_out, k2_out, vec_out, weight_two,
+                  pre, stats, taps, masks, k1_out, k2_out, vec_out,
                   kf, weight, acc, x, clips, sems, clip_sem, *frames):
     clip_copy = pltpu.make_async_copy(clips_in, clips, clip_sem)
     clip_copy.start()
@@ -374,8 +374,6 @@
         emit_pair(j)
         if j >= pairs and j % pairs == 0:
             convolve(j // pairs - 1)
-        if j == 4:
-            place_two(k2_out, weight_two)
     convolve(total // pairs - 1)
     spread(fold(acc[0]), fold(acc[1]), stats)
 
@@ -394,7 +392,6 @@
             like((9 * C_IN, C_MID), BF16),
             like((9 * C_MID, C_MID), BF16),
             like((4, C_MID), F32),
-            like((3 * WIDE, BOTH), BF16),
         ],
         [
             pltpu.VMEM((9 * (C_IN + C_MID), C_MID), F32),
@@ -446,8 +443,9 @@
                     weight[at : at + 128, to : to + 64] = turned
 
 
-def conv_two_body(count, pre_one, stats_one, vec, masks, k2, weight,
-                  pre, stats, taps, sums_out, weight_back, acc, *sides):
+def conv_two_body(count, pre_one, stats_one, vec, masks, k2,
+                  pre, stats, taps, sums_out, weight_back, acc, weight, *sides):
+    place_two(k2, weight)
     rows = masks.shape[1]
     half = rows - TAIL
     mels = 2
@@ -483,12 +481,12 @@
     spread(fold(acc[0]), fold(acc[1]), stats)
 
 
-def conv_two(pre_one, stats_one, vec, masks, k2, weight, count):
+def conv_two(pre_one, stats_one, vec, masks, k2, count):
     copies = stats_one.shape[0]
     rows = masks.shape[1]
     return call(
         lambda *refs: conv_two_body(count, *refs),
-        (pre_one, stats_one, vec, masks, k2, weight),
+        (pre_one, stats_one, vec, masks, k2),
         [
             like((MEL, rows, BOTH), F32),
             like((copies, 2, C_MID), F32),
@@ -496,7 +494,7 @@
             like((2, C_MID), F32),
             like((3 * WIDE, BOTH), BF16),
         ],
-        [pltpu.VMEM((2, 8, BOTH), F32), *side_scratch(rows)],
+        [pltpu.VMEM((2, 8, BOTH), F32), pltpu.VMEM((3 * WIDE, BOTH), BF16), *side_scratch(rows)],
     )
 
 
@@ -941,12 +939,12 @@
     up = lax.ppermute(up, AXES, [(i, i + 1) for i in range(ends)])
     down = lax.ppermute(down, AXES, [(i + 1, i) for i in range(ends)])
     weights = exchange(weights)
-    pre_one, stats, taps_x, masks, k1, k2, vec, weight = conv_one(
+    pre_one, stats, taps_x, masks, k1, k2, vec = conv_one(
         features, up, down, clips, weights, row_count
     )
     stats = exchange(stats)
     pre_two, stats, taps_a, sums_one, weight_back = conv_two(
-        pre_one, stats, vec, masks, k2, weight, count
+        pre_one, stats, vec, masks, k2, count
     )
     stats = exchange(stats)
     block_out, lift, stats, sums_two = norm_two(pre_two, stats, vec, cotangent, up, down, count)

time: 113 us -> 113 us (level)
  no operation moved by 1% of the time
where the time goes in v2:
time: 113 us; the launch traced here: 112 us
  Pallas kernels  45.6 us (40%)
  blocking collectives  36.1 us (32%)
  waiting for transfers between devices  15 us (13%)
  starting transfers between devices  14.9 us (13%)
    pallas_call x8, Pallas kernels, call(): pl.pallas_call(body, in_specs=in_specs or [VMEM] * len(args), out_specs=o...  45.6 us
    all_to_all x4, blocking collectives, exchange(): return lax.all_to_all(blocks, AXES, 0, 0, tiled=True)  36.1 us
    all_to_all x2, waiting for transfers between devices, exchange(): return lax.all_to_all(blocks, AXES, 0, 0, tiled=True)  10.1 us
    all_to_all x2, starting transfers between devices, exchange(): return lax.all_to_all(blocks, AXES, 0, 0, tiled=True)  9.91 us
    ppermute x1, starting transfers between devices, shards(): up = lax.ppermute(up, AXES, [(i, i + 1) for i in range(ends)])  3.67 us
    ppermute x1, waiting for transfers between devices, shards(): down = lax.ppermute(down, AXES, [(i + 1, i) for i in range(ends)])  3.31 us
  transfers between devices with their start and end apart: 4, of which 4 were waited for; matrix products, arithmetic and copies ran while one was open for 0% of the time, Pallas kernels for 9%

profile of v2, /device:TPU:0, one launch (start us, length us, event | category | flops | bytes accessed | tf_op | source)
XLA Modules:
  0.0 112.2 jit_solution(11552717244293978985)
XLA Ops:
  0.6 0.0 copy-start
  0.6 0.0 copy-start.2
  0.7 2.1 %shard_map.152 = (bf16[32,56,128]{2,1,0:T(8,128)(2,1)}, bf16[8,2048]{1,0:T(8,128)(2,1)}, bf16[8,2048]{1,0:T(8,128)(2,1)}) custom-call(bf16[32,72]{1,0:T(8,128)(2,1)} %bitcast.15, bf16[32,144]{1,0:T(8,128)(2,1)} %bitcast.14, bf16[1,32]{1,0:T(2,128)(2,1)} %bitcast.16, bf16[1,32]{1,0:T(2,128)(2,1)} %bitcast.17, bf16[1,32]{1,0:T(2,128)(2,1)} %bitcast.18, ...), custom_call_target="tpu_custom_call" | custom-call | flops 5000000000 | tf_op jit(solution)/shard_map/pallas_call | solution.py:33
  2.8 7.3 %all-to-all-start = ((bf16[32,56,128]{2,1,0:T(8,128)(2,1)}), bf16[32,56,128]{2,1,0:T(8,128)(2,1)S(1)}, u32[]{:S(2)}, u32[]{:S(2)}) async-start(bf16[32,56,128]{2,1,0:T(8,128)(2,1)} %get-tuple-element.42), calls=%async_computation | async-start | bytes 917504 | tf_op jit(solution)/shard_map/all_to_all | solution.py:923
  10.1 3.7 %collective-permute-start = (bf16[8,2048]{1,0:T(8,128)(2,1)}, bf16[8,2048]{1,0:T(8,128)(2,1)S(1)}, u32[]{:S(2)}, u32[]{:S(2)}) collective-permute-start(bf16[8,2048]{1,0:T(8,128)(2,1)} %get-tuple-element.40), channel_id=1, source_target_pairs={{0,1},{1,2},{2,3},{3,4},{4,5},{5,6},{6,7},{7,8},{8,9},{9,10},{10,1... | collective-permute-start | bytes 98312 | tf_op jit(solution)/shard_map/ppermute | solution.py:939
  13.8 1.3 %collective-permute-start.1 = (bf16[8,2048]{1,0:T(8,128)(2,1)}, bf16[8,2048]{1,0:T(8,128)(2,1)S(1)}, u32[]{:S(2)}, u32[]{:S(2)}) collective-permute-start(bf16[8,2048]{1,0:T(8,128)(2,1)} %get-tuple-element.41), channel_id=1, source_target_pairs={{1,0},{2,1},{3,2},{4,3},{5,4},{6,5},{7,6},{8,7},{9,8},{10,9},{11,1... | collective-permute-start | bytes 98312 | tf_op jit(solution)/shard_map/ppermute | solution.py:940
  15.1 1.5 %collective-permute-done.refs_1_.refs_4_ = bf16[8,2048]{1,0:T(8,128)(2,1)S(1)} collective-permute-done((bf16[8,2048]{1,0:T(8,128)(2,1)}, bf16[8,2048]{1,0:T(8,128)(2,1)S(1)}, u32[]{:S(2)}, u32[]{:S(2)}) %collective-permute-start) | collective-permute-done | bytes 32800 | tf_op jit(solution)/shard_map/ppermute | solution.py:939
  16.6 3.3 %collective-permute-done.1.refs_2_.refs_5_ = bf16[8,2048]{1,0:T(8,128)(2,1)S(1)} collective-permute-done((bf16[8,2048]{1,0:T(8,128)(2,1)}, bf16[8,2048]{1,0:T(8,128)(2,1)S(1)}, u32[]{:S(2)}, u32[]{:S(2)}) %collective-permute-start.1) | collective-permute-done | bytes 32800 | tf_op jit(solution)/shard_map/ppermute | solution.py:940
  19.9 5.5 %all-to-all-done.refs_4_ = bf16[32,56,128]{2,1,0:T(8,128)(2,1)S(1)} async-done(((bf16[32,56,128]{2,1,0:T(8,128)(2,1)}), bf16[32,56,128]{2,1,0:T(8,128)(2,1)S(1)}, u32[]{:S(2)}, u32[]{:S(2)}) %all-to-all-start) | async-done | bytes 458784 | tf_op jit(solution)/shard_map/all_to_all | solution.py:923
  25.4 0.0 copy-done
  25.4 0.0 copy-done.2
  25.4 4.9 %shard_map.153 = (f32[32,208,256]{2,1,0:T(8,128)S(1)}, f32[32,2,128]{2,1,0:T(2,128)S(1)}, bf16[18,208,512]{2,1,0:T(8,128)(2,1)S(1)}, f32[2,208,128]{2,1,0:T(8,12...) custom-call(bf16[384,2048]{1,0:T(8,128)(2,1)S(1)} %copy-done, ...), custom_call_target="tpu_custom_call" | custom-call | flops 5000000000 | tf_op jit(solution)/shard_map/pallas_call | solution.py:33
  30.4 9.5 %all_to_all.30.refs_1_ = f32[32,2,128]{2,1,0:T(2,128)S(1)} all-to-all(f32[32,2,128]{2,1,0:T(2,128)S(1)} %get-tuple-element.44), channel_id=1, replica_groups=mesh['grp'=4,'row'=8] {'grp','row'}, dimensions={0} | all-to-all | bytes 65536 | tf_op jit(solution)/shard_map/all_to_all | solution.py:923
  39.8 6.5 %shard_map.154 = (f32[32,208,256]{2,1,0:T(8,128)S(1)}, f32[32,2,128]{2,1,0:T(2,128)S(1)}, bf16[34,208,512]{2,1,0:T(8,128)(2,1)S(1)}, f32[2,128]{1,0:T(2,128)S(1)}, bf16[1536,256]{1,0:T(8,128)(2,1)S(1)}) custom-call(f32[32,208,256]{2,1,0:T(8,128)S(1)} %get-tuple-element.43.refs_0_.refs_7_.refs_1_, f32[32,2,128]{2,1,0:T(2,128)S(1)} %all_to_all.30.refs_1_, ...), custom_call_target="tpu_custom_call" | custom-call | flops 5000000000 | tf_op jit(solution)/shard_map/pallas_call | solution.py:33
  46.3 8.9 %all_to_all.31.refs_1_ = f32[32,2,128]{2,1,0:T(2,128)S(1)} all-to-all(f32[32,2,128]{2,1,0:T(2,128)S(1)} %get-tuple-element.49), channel_id=1, replica_groups=mesh['grp'=4,'row'=8] {'grp','row'}, dimensions={0} | all-to-all | bytes 65536 | tf_op jit(solution)/shard_map/all_to_all | solution.py:923
  55.2 4.0 %shard_map.155 = (bf16[192,2048]{1,0:T(8,128)(2,1)}, f32[32,208,256]{2,1,0:T(8,128)S(1)}, f32[32,2,128]{2,1,0:T(2,128)S(1)}, f32[2,128]{1,0:T(2,128)S(1)}) custom-call(f32[32,208,256]{2,1,0:T(8,128)S(1)} %get-tuple-element.48.refs_0_.refs_1_, f32[32,2,128]{2,1,0:T(2,128)S(1)} %all_to_all.31.refs_1_, f32[4,128]{1,0:T(4,128)S(1)} %get-tuple-element.45.refs_2_.refs_4_, ...), custom_call_target="tpu_custom_call" | custom-call | flops 5000000000 | tf_op jit(solution)/shard_map/pallas_call | solution.py:33
  59.2 8.9 %all_to_all.32.refs_3_ = f32[32,2,128]{2,1,0:T(2,128)S(1)} all-to-all(f32[32,2,128]{2,1,0:T(2,128)S(1)} %get-tuple-element.53), channel_id=1, replica_groups=mesh['grp'=4,'row'=8] {'grp','row'}, dimensions={0} | all-to-all | bytes 65536 | tf_op jit(solution)/shard_map/all_to_all | solution.py:923
  68.0 12.1 %shard_map.156 = (f32[32,208,256]{2,1,0:T(8,128)S(1)}, f32[128,1152]{1,0:T(8,128)S(1)}, f32[32,2,128]{2,1,0:T(2,128)S(1)}, f32[2,128]{1,0:T(2,128)S(1)}) custom-call(f32[32,208,256]{2,1,0:T(8,128)S(1)} %get-tuple-element.51.refs_0_, f32[32,208,256]{2,1,0:T(8,128)S(1)} %get-tuple-element.48.refs_0_.refs_1_, ...), custom_call_target="tpu_custom_call", output_to_operand_aliasing={{0}: (0, {})} | custom-call | flops 5000000000 | tf_op jit(solution)/shard_map/pallas_call | solution.py:33
  80.1 8.9 %all_to_all.33.refs_3_ = f32[32,2,128]{2,1,0:T(2,128)S(1)} all-to-all(f32[32,2,128]{2,1,0:T(2,128)S(1)} %get-tuple-element.58), channel_id=1, replica_groups=mesh['grp'=4,'row'=8] {'grp','row'}, dimensions={0} | all-to-all | bytes 65536 | tf_op jit(solution)/shard_map/all_to_all | solution.py:923
  89.0 4.8 %shard_map.157 = (bf16[640,208,256]{2,1,0:T(8,128)(2,1)}, bf16[32,56,128]{2,1,0:T(8,128)(2,1)}, f32[2,128]{1,0:T(2,128)S(1)}) custom-call(f32[32,208,256]{2,1,0:T(8,128)S(1)} %get-tuple-element.57.refs_0_, f32[32,208,256]{2,1,0:T(8,128)S(1)} %get-tuple-element.43.refs_0_.refs_7_.refs_1_, f32[2,128]{1,0:T(2,128)S(1)} %get-tuple-element.55.refs_8_.refs_2_, ...), custom_call_target="tpu_custom_call" | custom-call | flops 5000000000 | tf_op jit(solution)/shard_map/pallas_call | solution.py:33
  93.8 2.6 %all-to-all-start.5 = ((bf16[32,56,128]{2,1,0:T(8,128)(2,1)}), bf16[32,56,128]{2,1,0:T(8,128)(2,1)S(1)}, u32[]{:S(2)}, u32[]{:S(2)}) async-start(bf16[32,56,128]{2,1,0:T(8,128)(2,1)} %get-tuple-element.63), calls=%async_computation.5 | async-start | bytes 917504 | tf_op jit(solution)/shard_map/all_to_all | solution.py:923
  96.5 10.3 %shard_map.158 = f32[384,2048]{1,0:T(8,128)} custom-call(bf16[640,208,256]{2,1,0:T(8,128)(2,1)} %get-tuple-element.61.stored, bf16[576,128]{1,0:T(8,128)(2,1)S(1)} %get-tuple-element.62.k1), custom_call_target="tpu_custom_call" | custom-call | flops 5000000000 | tf_op jit(solution)/shard_map/pallas_call | solution.py:33
  106.8 4.6 %all-to-all-done.5.got = bf16[32,56,128]{2,1,0:T(8,128)(2,1)S(1)} async-done(((bf16[32,56,128]{2,1,0:T(8,128)(2,1)}), bf16[32,56,128]{2,1,0:T(8,128)(2,1)S(1)}, u32[]{:S(2)}, u32[]{:S(2)}) %all-to-all-start.5) | async-done | bytes 458784 | tf_op jit(solution)/shard_map/all_to_all | solution.py:923
  111.4 0.8 shard_map.159
  (2 shorter events, 0.0 us)
Async XLA Ops:
  0.6 24.8 %copy-start = (bf16[384,2048]{1,0:T(8,128)(2,1)S(1)}, bf16[384,2048]{1,0:T(8,128)(2,1)}, u32[]{:S(2)}) copy-start(bf16[384,2048]{1,0:T(8,128)(2,1)} %refs_0_.1) | copy-start | bytes 4718596
  0.6 24.8 %copy-start.2 = (s32[64]{0:T(128)S(1)}, s32[64]{0:T(128)}, u32[]{:S(2)}) copy-start(s32[64]{0:T(128)} %param.10) | copy-start | bytes 772
  2.8 22.6 %all-to-all-start = ((bf16[32,56,128]{2,1,0:T(8,128)(2,1)}), bf16[32,56,128]{2,1,0:T(8,128)(2,1)S(1)}, u32[]{:S(2)}, u32[]{:S(2)}) async-start(bf16[32,56,128]{2,1,0:T(8,128)(2,1)} %get-tuple-element.42), calls=%async_computation | async-start | bytes 917504 | tf_op jit(solution)/shard_map/all_to_all | solution.py:923
  10.1 6.5 %collective-permute-start = (bf16[8,2048]{1,0:T(8,128)(2,1)}, bf16[8,2048]{1,0:T(8,128)(2,1)S(1)}, u32[]{:S(2)}, u32[]{:S(2)}) collective-permute-start(bf16[8,2048]{1,0:T(8,128)(2,1)} %get-tuple-element.40), channel_id=1, source_target_pairs={{0,1},{1,2},{2,3},{3,4},{4,5},{5,6},{6,7},{7,8},{8,9},{9,10},{10,1... | collective-permute-start | bytes 98312 | tf_op jit(solution)/shard_map/ppermute | solution.py:939
  13.8 6.1 %collective-permute-start.1 = (bf16[8,2048]{1,0:T(8,128)(2,1)}, bf16[8,2048]{1,0:T(8,128)(2,1)S(1)}, u32[]{:S(2)}, u32[]{:S(2)}) collective-permute-start(bf16[8,2048]{1,0:T(8,128)(2,1)} %get-tuple-element.41), channel_id=1, source_target_pairs={{1,0},{2,1},{3,2},{4,3},{5,4},{6,5},{7,6},{8,7},{9,8},{10,9},{11,1... | collective-permute-start | bytes 98312 | tf_op jit(solution)/shard_map/ppermute | solution.py:940
  39.8 15.4 %copy-start.1 = (bf16[192,2048]{1,0:T(8,128)(2,1)S(1)}, bf16[192,2048]{1,0:T(8,128)(2,1)}, u32[]{:S(2)}) copy-start(bf16[192,2048]{1,0:T(8,128)(2,1)} %refs_3_.1) | copy-start | bytes 2359300
  93.8 17.6 %all-to-all-start.5 = ((bf16[32,56,128]{2,1,0:T(8,128)(2,1)}), bf16[32,56,128]{2,1,0:T(8,128)(2,1)S(1)}, u32[]{:S(2)}, u32[]{:S(2)}) async-start(bf16[32,56,128]{2,1,0:T(8,128)(2,1)} %get-tuple-element.63), calls=%async_computation.5 | async-start | bytes 917504 | tf_op jit(solution)/shard_map/all_to_all | solution.py:923
